TPU v7x, 32 devices: a whole 2x2x4 slice. The times are simulated.
32 devices in a mesh: section: 2 (over y), dp: 16 (over z, x, core).
Axes of the slice: x: 2, y: 2, z: 4, core: 2. Of those that a mesh axis runs over, the one named last changes fastest.
Arguments:
- tokens: bfloat16 [8192, 768], P('dp'), may hold values from -6 to 6
- cotangent: bfloat16 [8192, 768], P('dp'), may hold values from -6 to 6
- segments: int32 [32, 256], P('dp'), may hold values from 0 to 3, never falling along the last dimension, each value on 1 to 128 neighbouring positions
- chosen: int32 [32, 32], P('dp'), may hold values from 0 to 255, as said below
- router: float32 [768], replicated, may hold values from -0.21875 to 0.21875
- norm_gains: float32 [2, 2, 768], P('section'), may hold values from 0.1 to 1.9
- attn_in: bfloat16 [2, 3, 768, 768], P('section', None, 'dp'), may hold values from -0.21875 to 0.21875
- attn_out: bfloat16 [2, 768, 768], P('section', 'dp'), may hold values from -0.875 to 0.875
- ff_up: bfloat16 [2, 768, 3072], P('section', 'dp'), may hold values from -0.21875 to 0.21875
- ff_down: bfloat16 [2, 3072, 768], P('section', 'dp'), may hold values from -0.109375 to 0.109375
Outputs:
- ends: bfloat16 [2, 8192, 768], P('section', 'dp')
- router_grad: float32 [768], replicated
- gain_grad: float32 [2, 2, 768], P('section', None, 'dp')
- attn_in_grad: float32 [2, 3, 768, 768], P('section', None, 'dp')
- attn_out_grad: float32 [2, 768, 768], P('section', 'dp')
- up_grad: float32 [2, 768, 3072], P('section', 'dp')
- down_grad: float32 [2, 3072, 768], P('section', 'dp')
Inputs may be any that keep to these rules, and one draw needn't show every extreme that they name: `chosen`: each row holds 32 distinct positions of its sequence in increasing order.
All inputs are finite; a program needn't handle non-finite values.
Results may differ from a plain program's by a relative error of at most 0.014.
Values may be sent and summed in bfloat16 or wider, within the bound.
No kernel may reach another device: no remote copies, remote signals or barrier semaphores. Data moves between devices by JAX's collectives and lax.ppermute only.
A program may use at most 384 MiB of HBM per device.

v0:
```python
import jax
import jax.numpy as jnp
from jax import lax
from jax.sharding import PartitionSpec as P

HEAD_DIM = 64
MICRO = 2


EXACT_GELU_FLAG = lax.Precision.HIGHEST
EPSILON = 1e-05
MASKED = -1e30


def shifted(value, axis, by):
    size = lax.axis_size(axis)
    pairs = [(i, i + by) for i in range(size) if 0 <= i + by < size]
    return lax.ppermute(value, axis, pairs)


def normalize(rows, gain):
    inverse = lax.rsqrt(jnp.mean(rows * rows, axis=-1, keepdims=True) + EPSILON)
    normed = rows * inverse
    return (normed, inverse, normed * gain)


def norm_back(upstream, normed, inverse, gain):
    scaled = upstream * gain
    d_gain = jnp.sum(upstream * normed, axis=(0, 1))
    d_rows = inverse * (scaled - normed * jnp.mean(scaled * normed, axis=-1, keepdims=True))
    return (d_rows, d_gain)


def gelu_exact(value):
    return jax.nn.gelu(value, approximate=False)


def segment_mask(segment):
    order = lax.iota(jnp.int32, segment.shape[1])
    return (order[None, :, None] >= order[None, None, :]) & (
        segment[:, :, None] == segment[:, None, :]
    )


def masked_scores(query, keyed, mask):
    scores = jnp.einsum(
        "sqhd,skhd->shqk", query, keyed, preferred_element_type=jnp.float32
    ) * HEAD_DIM ** (-0.5)
    return jnp.where(mask[:, None], scores, MASKED)


def scatter_rows(base_line, spots, addition):
    return base_line.at[spots].add(addition)


def block_forward(rows, mask, gains, w_in, w_out, w_up, w_down):
    batch, count, width = rows.shape
    normed_one, inverse_one, pre_one = normalize(rows, gains[0])
    act_one = pre_one.astype(jnp.bfloat16)
    projected = jnp.einsum(
        "srd,cde->csre", act_one, w_in, preferred_element_type=jnp.float32
    ).astype(jnp.bfloat16)
    projected = projected.reshape(3, batch, count, width // HEAD_DIM, HEAD_DIM)
    scores = masked_scores(projected[0], projected[1], mask)
    top = jnp.max(scores, axis=-1, keepdims=True)
    powers = jnp.exp(scores - top)
    total = jnp.sum(powers, axis=-1, keepdims=True)
    chances = (powers / total).astype(jnp.bfloat16)
    mixed = jnp.einsum("shqk,skhd->sqhd", chances, projected[2], preferred_element_type=jnp.float32)
    mixed = mixed.reshape(batch, count, width).astype(jnp.bfloat16)
    attended = jnp.einsum("srd,de->sre", mixed, w_out, preferred_element_type=jnp.float32)
    intermediate_hidden = rows + attended
    normed_two, inverse_two, pre_two = normalize(intermediate_hidden, gains[1])
    act_two = pre_two.astype(jnp.bfloat16)
    upped = jnp.einsum("srd,df->srf", act_two, w_up, preferred_element_type=jnp.float32)
    hidden = gelu_exact(upped).astype(jnp.bfloat16)
    branch = attended + jnp.einsum(
        "srf,fd->srd", hidden, w_down, preferred_element_type=jnp.float32
    )
    log_total = top + jnp.log(total)
    saved = (
        normed_one,
        inverse_one,
        act_one,
        projected,
        log_total,
        mixed,
        normed_two,
        inverse_two,
        act_two,
        upped,
        hidden,
    )
    return (branch, saved)


def block_backward(grad_branch, mask, saved, gains, w_in, w_out, w_up, w_down):
    (
        normed_one,
        inverse_one,
        act_one,
        projected,
        log_total,
        mixed,
        normed_two,
        inverse_two,
        act_two,
        upped,
        hidden,
    ) = saved
    batch, count, width = grad_branch.shape
    d_out = grad_branch.astype(jnp.bfloat16)
    g_down = jnp.einsum("srf,srd->fd", hidden, d_out, preferred_element_type=jnp.float32)
    d_hidden = jnp.einsum("srd,fd->srf", d_out, w_down, preferred_element_type=jnp.float32)
    d_upped = jax.vjp(gelu_exact, upped)[1](d_hidden)[0].astype(jnp.bfloat16)
    g_up = jnp.einsum("srd,srf->df", act_two, d_upped, preferred_element_type=jnp.float32)
    d_act_two = jnp.einsum("srf,df->srd", d_upped, w_up, preferred_element_type=jnp.float32)
    d_middle, g_gain_two = norm_back(d_act_two, normed_two, inverse_two, gains[1])
    d_attended = (grad_branch + d_middle).astype(jnp.bfloat16)
    g_out = jnp.einsum("srd,sre->de", mixed, d_attended, preferred_element_type=jnp.float32)
    d_mixed = jnp.einsum(
        "sre,de->srd", d_attended, w_out, preferred_element_type=jnp.float32
    ).astype(jnp.bfloat16)
    d_mixed = d_mixed.reshape(batch, count, width // HEAD_DIM, HEAD_DIM)
    chances = jnp.exp(masked_scores(projected[0], projected[1], mask) - log_total)
    d_chances = jnp.einsum(
        "sqhd,skhd->shqk", d_mixed, projected[2], preferred_element_type=jnp.float32
    )
    d_value = jnp.einsum(
        "shqk,sqhd->skhd", chances.astype(jnp.bfloat16), d_mixed, preferred_element_type=jnp.float32
    )
    d_scores = chances * (d_chances - jnp.sum(chances * d_chances, axis=-1, keepdims=True))
    d_scores = d_scores.astype(jnp.bfloat16)
    factor = HEAD_DIM ** (-0.5)
    d_query = (
        jnp.einsum("shqk,skhd->sqhd", d_scores, projected[1], preferred_element_type=jnp.float32)
        * factor
    )
    d_key = (
        jnp.einsum("shqk,sqhd->skhd", d_scores, projected[0], preferred_element_type=jnp.float32)
        * factor
    )
    d_projected = (
        jnp.stack([d_query, d_key, d_value]).reshape(3, batch, count, width).astype(jnp.bfloat16)
    )
    g_in = jnp.einsum("srd,csre->cde", act_one, d_projected, preferred_element_type=jnp.float32)
    d_act_one = jnp.einsum("csre,cde->srd", d_projected, w_in, preferred_element_type=jnp.float32)
    d_rows, g_gain_one = norm_back(d_act_one, normed_one, inverse_one, gains[0])
    return (d_rows + d_middle, (g_in, g_out, g_up, g_down, jnp.stack([g_gain_one, g_gain_two])))


def on_section(active, work, *operands):

    def skipped(*inner):
        return jax.tree.map(jnp.zeros_like, work(*inner))

    return lax.cond(active, work, skipped, *operands)


def body(
    tokens, cotangent, segments, chosen, router, norm_gains, attn_in, attn_out, ff_up, ff_down
):
    full_in, full_out, full_up, full_down = (
        lax.all_gather(attn_in, "dp", axis=2, tiled=True),
        lax.all_gather(attn_out, "dp", axis=1, tiled=True),
        lax.all_gather(ff_up, "dp", axis=1, tiled=True),
        lax.all_gather(ff_down, "dp", axis=1, tiled=True),
    )
    weights = (full_in[0], full_out[0], full_up[0], full_down[0])
    gains = norm_gains[0]
    routed = lax.axis_index("section") == 0
    length = segments.shape[1]
    per_micro = segments.shape[0] // MICRO
    width = tokens.shape[1]
    inputs = tokens.reshape(MICRO, per_micro, length, width)
    upstream = cotangent.reshape(MICRO, per_micro, length, width)
    seg_blocks = segments.reshape(MICRO, per_micro, length)
    pick_blocks = chosen.reshape(MICRO, per_micro, -1)

    def selection(segment, picked_at):
        one_hot_selection = (
            picked_at[:, :, None] == lax.iota(jnp.int32, length)[None, None, :]
        ).astype(jnp.bfloat16)
        return (one_hot_selection, segment_mask(jnp.take_along_axis(segment, picked_at, axis=1)))

    def routed_forward(rows_per_block, segment, picked_at):
        one_hot_selection, mask = selection(segment, picked_at)
        routed_token_rows = jnp.einsum(
            "wgo,woq->wgq", one_hot_selection, rows_per_block, preferred_element_type=jnp.float32
        )
        gate = jax.nn.sigmoid(
            jnp.einsum("skd,d->sk", routed_token_rows, router, precision=EXACT_GELU_FLAG)
        )
        branch, saved = block_forward(routed_token_rows, mask, gains, *weights)
        residual_update = (gate[..., None] * branch).astype(jnp.bfloat16)
        return (residual_update, (routed_token_rows, gate, branch, saved))

    def routed_delta(rows_per_block, segment, picked_at):
        return routed_forward(rows_per_block, segment, picked_at)[0]

    def dense_work(rows_per_block, segment, picked_at, arrived, grad_out):
        base = jax.vmap(scatter_rows)(
            rows_per_block.astype(jnp.float32), picked_at, arrived.astype(jnp.float32)
        )
        mask = segment_mask(segment)
        branch, saved = block_forward(base, mask, gains, *weights)
        result = (base + branch).astype(jnp.bfloat16)
        grad_full = grad_out.astype(jnp.float32)
        d_rows, grads = block_backward(grad_full, mask, saved, gains, *weights)
        return (result, (grad_full + d_rows).astype(jnp.bfloat16), grads)

    def routed_back(segment, picked_at, returned_outputs, stash):
        one_hot_selection, mask = selection(segment, picked_at)
        routed_token_rows, gate, branch, saved = stash
        residual_update_gradient = jnp.einsum(
            "wgo,woq->wgq", one_hot_selection, returned_outputs, preferred_element_type=jnp.float32
        )
        d_logit = jnp.sum(residual_update_gradient * branch, axis=-1) * gate * (1.0 - gate)
        d_picked, grads = block_backward(
            gate[..., None] * residual_update_gradient, mask, saved, gains, *weights
        )
        d_picked = d_picked + d_logit[..., None] * router
        g_router = jnp.einsum("sk,skd->d", d_logit, routed_token_rows, precision=EXACT_GELU_FLAG)
        d_input = jax.vmap(scatter_rows)(returned_outputs.astype(jnp.float32), picked_at, d_picked)
        return (d_input.astype(jnp.bfloat16), grads, g_router)

    def routed_back_again(rows_per_block, segment, picked_at, returned_outputs):
        stash = routed_forward(rows_per_block, segment, picked_at)[1]
        return routed_back(segment, picked_at, returned_outputs, stash)

    arrivals = []
    for micro in range(MICRO):
        residual_update = on_section(
            routed, routed_delta, inputs[micro], seg_blocks[micro], pick_blocks[micro]
        )
        arrivals.append(shifted(residual_update, "section", 1))
    results = []
    returns = []
    dense_grads = []
    for micro in range(MICRO):
        result, back, grads = on_section(
            jnp.logical_not(routed),
            dense_work,
            inputs[micro],
            seg_blocks[micro],
            pick_blocks[micro],
            arrivals[micro],
            upstream[micro],
        )
        results.append(result)
        dense_grads.append(grads)
        returns.append(shifted(back, "section", -1))
    input_grads = []
    router_total = jnp.zeros_like(router)
    summed = None
    for micro in range(MICRO):
        d_input, grads, g_router = on_section(
            routed,
            routed_back_again,
            inputs[micro],
            seg_blocks[micro],
            pick_blocks[micro],
            returns[micro],
        )
        input_grads.append(d_input)
        router_total = router_total + g_router
        combined = jax.tree.map(jnp.add, grads, dense_grads[micro])
        summed = combined if summed is None else jax.tree.map(jnp.add, summed, combined)
    summed = (
        lax.psum_scatter(summed[0][None], "dp", scatter_dimension=2, tiled=True),
        lax.psum_scatter(summed[1][None], "dp", scatter_dimension=1, tiled=True),
        lax.psum_scatter(summed[2][None], "dp", scatter_dimension=1, tiled=True),
        lax.psum_scatter(summed[3][None], "dp", scatter_dimension=1, tiled=True),
        lax.psum_scatter(summed[4][None], "dp", scatter_dimension=2, tiled=True),
    )
    router_grad = lax.psum(router_total, ("section", "dp"))
    first_rows = jnp.stack(input_grads).reshape(-1, width)
    second_rows = jnp.stack(results).reshape(-1, width)
    ends = jnp.where(routed, first_rows, second_rows)[None]
    return (ends, router_grad, summed[4], summed[0], summed[1], summed[2], summed[3])


def solution(mesh):
    return jax.shard_map(
        body,
        mesh=mesh,
        in_specs=(
            P("dp", None),
            P("dp", None),
            P("dp", None),
            P("dp", None),
            P(),
            P("section", None, None),
            P("section", None, "dp", None),
            P("section", "dp", None),
            P("section", "dp", None),
            P("section", "dp", None),
        ),
        out_specs=(
            P("section", "dp", None),
            P(),
            P("section", None, "dp"),
            P("section", None, "dp", None),
            P("section", "dp", None),
            P("section", "dp", None),
            P("section", "dp", None),
        ),
        check_vma=False,
    )
```

profile of v0, /device:TPU:0, one launch (start us, length us, event | category | flops | bytes accessed | tf_op | source)
XLA Modules:
  0.0 928.5 jit_solution(4360732975516417422)
XLA Ops:
  13.3 38.0 %all-gather.7.cloned.1.call-done = bf16[1,768,768]{2,1,0:T(8,128)(2,1)} async-done(((bf16[1,48,768]{2,1,0:T(8,128)(2,1)}), bf16[1,768,768]{2,1,0:T(8,128)(2,1)}) %all-gather.7.cloned.1.call-update) | async-done | bytes 1179664 | tf_op jit(solution)/shard_map/all_gather | solution.py:165
  51.3 48.5 %all-gather.5.cloned.1.call-done = bf16[1,3,768,768]{3,2,1,0:T(8,128)(2,1)} async-done(((bf16[1,3,48,768]{3,2,1,0:T(8,128)(2,1)}), bf16[1,3,768,768]{3,2,1,0:T(8,128)(2,1)}) %all-gather.5.cloned.1.call-update) | async-done | bytes 3538960 | tf_op jit(solution)/shard_map/all_gather | solution.py:164
  99.8 54.5 %all-gather.9.cloned.1.call-done = bf16[1,768,3072]{2,1,0:T(8,128)(2,1)} async-done(((bf16[1,48,3072]{2,1,0:T(8,128)(2,1)}), bf16[1,768,3072]{2,1,0:T(8,128)(2,1)}) %all-gather.9.cloned.1.call-update) | async-done | bytes 4718608 | tf_op jit(solution)/shard_map/all_gather | solution.py:166
  154.4 54.0 %all-gather.11.cloned.1.call-done = bf16[1,3072,768]{2,1,0:T(8,128)(2,1)} async-done(((bf16[1,192,768]{2,1,0:T(8,128)(2,1)}), bf16[1,3072,768]{2,1,0:T(8,128)(2,1)}) %all-gather.11.cloned.1.call-update) | async-done | bytes 4718608 | tf_op jit(solution)/shard_map/all_gather | solution.py:167
  208.3 14.0 %conditional.9 = (bf16[1,32,768]{2,1,0:T(8,128)(2,1)S(1)}) conditional(s32[]{:T(128)} %convert_element_type.454, () %tuple.69, (s32[1,1,32]{2,1,0:T(1,128)}, bf16[1,256,768]{2,1,0:T(8,128)(2,1)S(1)}, f32[768]{0:T(1024)}, f32[2,768]{1,0:T(2,128)}, bf16[3,768,768]{2,1,0:T(8,128)(2,1)}, /*index=5*/s32[1,256]{1,0:T(1,128)S(1)}, ...), branch_computations={%region_31.33_spmd, %region_32.38_spmd} | conditional | flops 475927040 | bytes 21420708 | solution.py:157
  216.3 6.0 fusion.298
  223.6 13.9 %conditional.6 = (bf16[1,32,768]{2,1,0:T(8,128)(2,1)}) conditional(s32[]{:T(128)} %convert_element_type.454, () %tuple.63, (s32[1,1,32]{2,1,0:T(1,128)S(1)}, bf16[1,256,768]{2,1,0:T(8,128)(2,1)S(1)}, f32[768]{0:T(1024)}, f32[2,768]{1,0:T(2,128)}, bf16[3,768,768]{2,1,0:T(8,128)(2,1)}, /*index=5*/s32[1,256]{1,0:T(1,128)S(1)}, s32[1,32]{1,0:T(1,128)S(1)}, ...), branch_computations={%region_0.0_spmd, %region_1.7_spmd} | conditional | flops 475927040 | bytes 21420708 | solution.py:157
  231.0 6.6 fusion.122
  239.5 14.1 %conditional.10 = (bf16[1,256,768]{2,1,0:T(8,128)(2,1)}, f32[768,768]{1,0:T(8,128)S(1)}, f32[768,3072]{1,0:T(8,128)}, f32[3072,768]{1,0:T(8,128)S(1)}, f32[2,768...) conditional(s32[]{:T(128)} %convert_element_type.455, () %tuple.68, ...), branch_computations={%region_37.39_spmd, %region_38.50_spmd} | conditional | flops 11566491648 | bytes 293867808 | solution.py:157
  245.9 4.9 broadcast.1623
  257.8 15.1 %conditional.7 = (bf16[1,256,768]{2,1,0:T(8,128)(2,1)}, f32[768,768]{1,0:T(8,128)S(1)}, f32[768,3072]{1,0:T(8,128)S(1)}, f32[3072,768]{1,0:T(8,128)S(1)}, f32[2,...) conditional(s32[]{:T(128)} %convert_element_type.455, () %tuple.62, ...), branch_computations={%region_6.0_spmd, %region_7.19_spmd} | conditional | flops 11566491648 | bytes 293892448 | solution.py:157
  274.3 37.0 %collective-permute-done.3 = bf16[1,256,768]{2,1,0:T(8,128)(2,1)} collective-permute-done((bf16[1,256,768]{2,1,0:T(8,128)(2,1)}, bf16[1,256,768]{2,1,0:T(8,128)(2,1)}, u32[]{:S(2)}, u32[]{:S(2)}) %collective-permute-start.3) | collective-permute-done | bytes 393248 | tf_op jit(solution)/shard_map/ppermute | solution.py:18
  311.4 74.8 %conditional.11 = (f32[768,768]{1,0:T(8,128)}, f32[768,3072]{1,0:T(8,128)S(1)}, f32[3072,768]{1,0:T(8,128)S(1)}, f32[2,768]{1,0:T(2,128)}, f32[768]{0:T(1024)}, ...) conditional(s32[]{:T(128)} %convert_element_type.454, () %tuple.67, (s32[1,1,32]{2,1,0:T(1,128)}, ...), branch_computations={%region_49.51_spmd, %region_50.63_spmd} | conditional | flops 1404206848 | bytes 144657024 | solution.py:157
  324.8 4.7 multiply_convert_fusion.33
  360.3 3.8 scatter_custom_fusion.3
  370.8 4.0 convolution_bitcast_fusion.7
  374.8 8.2 copy.238
  392.6 81.1 %conditional.8 = (f32[768,768]{1,0:T(8,128)}, f32[768,3072]{1,0:T(8,128)}, f32[3072,768]{1,0:T(8,128)}, f32[2,768]{1,0:T(2,128)S(1)}, f32[768]{0:T(1024)S(1)}, /...) conditional(s32[]{:T(128)} %convert_element_type.454, () %tuple.61, (s32[1,1,32]{2,1,0:T(1,128)}, ...), branch_computations={%region_18.20_spmd, %region_19.32_spmd} | conditional | flops 1404206848 | bytes 144681632 | solution.py:157
  405.8 4.7 multiply_convert_fusion.15
  451.2 4.0 convolution_bitcast_fusion.3
  455.2 8.1 copy.234
  463.4 5.0 fusion.288
  468.4 5.1 fusion.286
  475.5 5.8 add_bitcast_fusion.3
  481.4 13.4 %add_bitcast_fusion.2 = f32[1,3,768,768]{3,2,1,0:T(8,128)} fusion(f32[3,768,768]{2,1,0:T(8,128)} %get-tuple-element.269, f32[3,768,768]{2,1,0:T(8,128)} %get-tuple-element.268, f32[3,768,768]{2,1,0:T(8,128)} %get-tuple-element.267, f32[3,768,768]{2,1,0:T(8,128)} %get-tuple-element.266), kind=kLoop, calls=%fused_computation.718 | loop fusion | flops 5308416 | bytes 35389440 | tf_op jit(solution)/shard_map/broadcast_in_dim | solution.py:270
  494.8 17.4 %add_bitcast_fusion.1 = f32[1,768,3072]{2,1,0:T(8,128)} fusion(f32[768,3072]{1,0:T(8,128)} %copy-done.16, f32[768,3072]{1,0:T(8,128)} %get-tuple-element.261, f32[768,3072]{1,0:T(8,128)} %get-tuple-element.258, f32[768,3072]{1,0:T(8,128)} %copy-done.14), kind=kLoop, calls=%fused_computation.717 | loop fusion | flops 7077888 | bytes 47185920 | tf_op jit(solution)/shard_map/broadcast_in_dim | solution.py:272
  512.3 17.0 %add_bitcast_fusion = f32[1,3072,768]{2,1,0:T(8,128)} fusion(f32[3072,768]{1,0:T(8,128)} %copy-done.15, f32[3072,768]{1,0:T(8,128)} %copy-done.12, f32[3072,768]{1,0:T(8,128)} %get-tuple-element.262, f32[3072,768]{1,0:T(8,128)} %copy-done.13), kind=kLoop, calls=%fused_computation.716 | loop fusion | flops 7077888 | bytes 47185920 | tf_op jit(solution)/shard_map/broadcast_in_dim | solution.py:273
  529.9 39.3 %psum.7 = f32[768]{0:T(1024)} all-reduce(f32[768]{0:T(1024)S(1)} %add.332), channel_id=1, replica_groups=mesh['section'=2,'dp'=16] {'section','dp'}, use_global_device_ids=true, to_apply=%region_62.64 | all-reduce | flops 768 | bytes 6144 | tf_op jit(solution)/shard_map/psum | solution.py:276
  572.7 23.3 %reduce-scatter.10.cloned.1.call-done = f32[1,48,768]{2,1,0:T(8,128)} async-done(((f32[1,768,768]{2,1,0:T(8,128)}), f32[1,48,768]{2,1,0:T(8,128)}) %reduce-scatter.10.cloned.1.call-update) | async-done | bytes 147472 | tf_op jit(solution)/shard_map/reduce_scatter | solution.py:271
  596.0 93.7 %reduce-scatter.8.cloned.1.call-done = f32[1,3,48,768]{3,2,1,0:T(8,128)} async-done(((f32[1,3,768,768]{3,2,1,0:T(8,128)}), f32[1,3,48,768]{3,2,1,0:T(8,128)}) %reduce-scatter.8.cloned.1.call-update) | async-done | bytes 442384 | tf_op jit(solution)/shard_map/reduce_scatter | solution.py:270
  689.7 116.1 %reduce-scatter.12.cloned.1.call-done = f32[1,48,3072]{2,1,0:T(8,128)} async-done(((f32[1,768,3072]{2,1,0:T(8,128)}), f32[1,48,3072]{2,1,0:T(8,128)}) %reduce-scatter.12.cloned.1.call-update) | async-done | bytes 589840 | tf_op jit(solution)/shard_map/reduce_scatter | solution.py:272
  805.8 115.8 %reduce-scatter.14.cloned.1.call-done = f32[1,192,768]{2,1,0:T(8,128)} async-done(((f32[1,3072,768]{2,1,0:T(8,128)}), f32[1,192,768]{2,1,0:T(8,128)}) %reduce-scatter.14.cloned.1.call-update) | async-done | bytes 589840 | tf_op jit(solution)/shard_map/reduce_scatter | solution.py:273
  (392 shorter events, 163.0 us)
Async XLA Ops:
  7.2 44.2 %all-gather.7.cloned.1.call-start = ((), (), s32[]{:S(2)}) async-start(), calls=%async_computation.6 | async-start | bytes 1253376 | tf_op jit(solution)/shard_map/all_gather | solution.py:165
  7.9 91.9 %all-gather.5.cloned.1.call-start = ((), (), s32[]{:S(2)}) async-start(), calls=%async_computation.5 | async-start | bytes 3760128 | tf_op jit(solution)/shard_map/all_gather | solution.py:164
  8.6 145.7 %all-gather.9.cloned.1.call-start = ((), (), s32[]{:S(2)}) async-start(), calls=%async_computation.7 | async-start | bytes 5013504 | tf_op jit(solution)/shard_map/all_gather | solution.py:166
  9.4 199.0 %all-gather.11.cloned.1.call-start = ((), (), s32[]{:S(2)}) async-start(), calls=%async_computation.8 | async-start | bytes 5013504 | tf_op jit(solution)/shard_map/all_gather | solution.py:167
  10.0 561.4 %reduce-scatter.16.cloned.1.call-start = ((), (), s32[]{:S(2)}) async-start(), calls=%async_computation.13 | async-start | bytes 417792
  11.3 212.3 %copy-start.153 = (s32[1,1,32]{2,1,0:T(1,128)}, s32[1,1,32]{2,1,0:T(1,128)S(1)}, u32[]{:S(2)}) copy-start(s32[1,1,32]{2,1,0:T(1,128)S(1)} %get-tuple-element.395) | copy-start | bytes 388
  11.3 212.3 %copy-start.158 = (s32[1,32]{1,0:T(1,128)}, s32[1,32]{1,0:T(1,128)S(1)}, u32[]{:S(2)}) copy-start(s32[1,32]{1,0:T(1,128)S(1)} %get-tuple-element.394) | copy-start | bytes 388
  11.3 228.1 %copy-start.159 = (s32[1,32]{1,0:T(1,128)}, s32[1,32]{1,0:T(1,128)S(1)}, u32[]{:S(2)}) copy-start(s32[1,32]{1,0:T(1,128)S(1)} %get-tuple-element.397) | copy-start | bytes 388
  13.3 210.3 %copy-start.45 = (bf16[1,256,768]{2,1,0:T(8,128)(2,1)}, bf16[1,256,768]{2,1,0:T(8,128)(2,1)S(1)}, u32[]{:S(2)}) copy-start(bf16[1,256,768]{2,1,0:T(8,128)(2,1)S(1)} %get-tuple-element.390) | copy-start | bytes 1179652
  13.3 226.2 %copy-start.46 = (bf16[1,256,768]{2,1,0:T(8,128)(2,1)}, bf16[1,256,768]{2,1,0:T(8,128)(2,1)S(1)}, u32[]{:S(2)}) copy-start(bf16[1,256,768]{2,1,0:T(8,128)(2,1)S(1)} %get-tuple-element.391) | copy-start | bytes 1179652
  222.3 17.2 %collective-permute-start.2 = (bf16[1,32,768]{2,1,0:T(8,128)(2,1)S(1)}, bf16[1,32,768]{2,1,0:T(8,128)(2,1)S(1)}, u32[]{:S(2)}, u32[]{:S(2)}) collective-permute-start(bf16[1,32,768]{2,1,0:T(8,128)(2,1)S(1)} %get-tuple-element.455), channel_id=1, source_target_pairs={{0,16},{1,17},{2,18},{3,19},{4,20},{5,21},{6,22},{7,23},{8,24},{9,... | collective-permute-start | bytes 147464 | tf_op jit(solution)/shard_map/ppermute | solution.py:18
  237.6 17.4 %collective-permute-start = (bf16[1,32,768]{2,1,0:T(8,128)(2,1)}, bf16[1,32,768]{2,1,0:T(8,128)(2,1)}, u32[]{:S(2)}, u32[]{:S(2)}) collective-permute-start(bf16[1,32,768]{2,1,0:T(8,128)(2,1)} %get-tuple-element.454), channel_id=1, source_target_pairs={{0,16},{1,17},{2,18},{3,19},{4,20},{5,21},{6,22},{7,23},{8,24},{9,... | collective-permute-start | bytes 147464 | tf_op jit(solution)/shard_map/ppermute | solution.py:18
  253.6 57.7 %collective-permute-start.3 = (bf16[1,256,768]{2,1,0:T(8,128)(2,1)}, bf16[1,256,768]{2,1,0:T(8,128)(2,1)}, u32[]{:S(2)}, u32[]{:S(2)}) collective-permute-start(bf16[1,256,768]{2,1,0:T(8,128)(2,1)} %get-tuple-element.240), channel_id=1, source_target_pairs={{16,0},{17,1},{18,2},{19,3},{20,4},{21,5},{22,6},{23,7},{24,8},{25... | collective-permute-start | bytes 1179656 | tf_op jit(solution)/shard_map/ppermute | solution.py:18
  254.9 56.4 %copy-start.120 = (f32[768]{0:T(1024)S(1)}, f32[768]{0:T(1024)}, u32[]{:S(2)}) copy-start(f32[768]{0:T(1024)} %param.28) | copy-start | bytes 9220
  273.0 38.4 %copy-start.32 = (f32[768,768]{1,0:T(8,128)}, f32[768,768]{1,0:T(8,128)S(1)}, u32[]{:S(2)}) copy-start(f32[768,768]{1,0:T(8,128)S(1)} %get-tuple-element.255) | copy-start | bytes 7077892
  273.0 38.4 %copy-start.13 = (f32[3072,768]{1,0:T(8,128)}, f32[3072,768]{1,0:T(8,128)S(1)}, u32[]{:S(2)}) copy-start(f32[3072,768]{1,0:T(8,128)S(1)} %get-tuple-element.263) | copy-start | bytes 28311556
  273.0 38.4 %copy-start.14 = (f32[768,3072]{1,0:T(8,128)}, f32[768,3072]{1,0:T(8,128)S(1)}, u32[]{:S(2)}) copy-start(f32[768,3072]{1,0:T(8,128)S(1)} %get-tuple-element.259) | copy-start | bytes 28311556
  273.0 113.9 %collective-permute-start.1 = (bf16[1,256,768]{2,1,0:T(8,128)(2,1)}, bf16[1,256,768]{2,1,0:T(8,128)(2,1)}, u32[]{:S(2)}, u32[]{:S(2)}) collective-permute-start(bf16[1,256,768]{2,1,0:T(8,128)(2,1)} %get-tuple-element.238), channel_id=1, source_target_pairs={{16,0},{17,1},{18,2},{19,3},{20,4},{21,5},{22,6},{23,7},{24,8},{25... | collective-permute-start | bytes 1179656 | tf_op jit(solution)/shard_map/ppermute | solution.py:18
  312.7 17.8 %copy-start.39 = (f32[32,768]{1,0:T(8,128)}, f32[32,768]{1,0:T(8,128)S(1)}, u32[]{:S(2)}) copy-start(f32[32,768]{1,0:T(8,128)S(1)} %get-tuple-element.379) | copy-start | bytes 294916 | tf_op jit(solution)/shard_map/cond
  317.5 13.3 %copy-start.69 = (f32[32,768]{1,0:T(8,128)}, f32[32,768]{1,0:T(8,128)S(1)}, u32[]{:S(2)}) copy-start(f32[32,768]{1,0:T(8,128)S(1)} %fusion.410) | copy-start | bytes 294916 | tf_op jit(solution)/shard_map/cond
  322.6 12.7 %copy-start.61 = (f32[32,768]{1,0:T(8,128)}, f32[32,768]{1,0:T(8,128)S(1)}, u32[]{:S(2)}) copy-start(f32[32,768]{1,0:T(8,128)S(1)} %get-tuple-element.317) | copy-start | bytes 294916 | tf_op jit(solution)/shard_map/cond
  333.9 23.0 %copy-start.2 = (bf16[3,768,768]{2,1,0:T(8,128)(2,1)S(1)}, bf16[3,768,768]{2,1,0:T(8,128)(2,1)}, u32[]{:S(2)}) copy-start(bf16[3,768,768]{2,1,0:T(8,128)(2,1)} %get-tuple-element.195) | copy-start | bytes 10616836 | tf_op jit(solution)/shard_map/cond
  394.0 17.6 %copy-start.42 = (f32[32,768]{1,0:T(8,128)}, f32[32,768]{1,0:T(8,128)S(1)}, u32[]{:S(2)}) copy-start(f32[32,768]{1,0:T(8,128)S(1)} %get-tuple-element.362) | copy-start | bytes 294916 | tf_op jit(solution)/shard_map/cond
  398.5 13.3 %copy-start.72 = (f32[32,768]{1,0:T(8,128)}, f32[32,768]{1,0:T(8,128)S(1)}, u32[]{:S(2)}) copy-start(f32[32,768]{1,0:T(8,128)S(1)} %fusion.234) | copy-start | bytes 294916 | tf_op jit(solution)/shard_map/cond
  415.0 22.6 %copy-start.3 = (bf16[3,768,768]{2,1,0:T(8,128)(2,1)S(1)}, bf16[3,768,768]{2,1,0:T(8,128)(2,1)}, u32[]{:S(2)}) copy-start(bf16[3,768,768]{2,1,0:T(8,128)(2,1)} %get-tuple-element.164) | copy-start | bytes 10616836 | tf_op jit(solution)/shard_map/cond
  475.5 120.6 %reduce-scatter.10.cloned.1.call-start = ((), (), s32[]{:S(2)}) async-start(), calls=%async_computation.10 | async-start | bytes 2506752 | tf_op jit(solution)/shard_map/reduce_scatter | solution.py:271
  481.3 208.4 %reduce-scatter.8.cloned.1.call-start = ((), (), s32[]{:S(2)}) async-start(), calls=%async_computation.9 | async-start | bytes 7520256 | tf_op jit(solution)/shard_map/reduce_scatter | solution.py:270
  494.8 311.1 %reduce-scatter.12.cloned.1.call-start = ((), (), s32[]{:S(2)}) async-start(), calls=%async_computation.11 | async-start | bytes 10027008 | tf_op jit(solution)/shard_map/reduce_scatter | solution.py:272
  512.2 409.5 %reduce-scatter.14.cloned.1.call-start = ((), (), s32[]{:S(2)}) async-start(), calls=%async_computation.12 | async-start | bytes 10027008 | tf_op jit(solution)/shard_map/reduce_scatter | solution.py:273
  529.3 40.0 %copy-start.95 = (bf16[1,1,256,768]{3,2,1,0:T(8,128)(2,1)S(1)}, bf16[1,1,256,768]{3,2,1,0:T(8,128)(2,1)}, u32[]{:S(2)}) copy-start(bf16[1,1,256,768]{3,2,1,0:T(8,128)(2,1)} %get-tuple-element.243) | copy-start | bytes 1179652
  529.3 40.0 %copy-start.96 = (bf16[1,1,256,768]{3,2,1,0:T(8,128)(2,1)S(1)}, bf16[1,1,256,768]{3,2,1,0:T(8,128)(2,1)}, u32[]{:S(2)}) copy-start(bf16[1,1,256,768]{3,2,1,0:T(8,128)(2,1)} %get-tuple-element.242) | copy-start | bytes 1179652
  529.3 40.0 %copy-start.97 = (bf16[1,1,256,768]{3,2,1,0:T(8,128)(2,1)S(1)}, bf16[1,1,256,768]{3,2,1,0:T(8,128)(2,1)}, u32[]{:S(2)}) copy-start(bf16[1,1,256,768]{3,2,1,0:T(8,128)(2,1)} %get-tuple-element.241) | copy-start | bytes 1179652
  (73 other events, 371.0 us)
Sparse Core Ops, SparseCore 0:
  10.3 41.0 all-gather.6
  53.6 46.1 all-gather.4
  102.1 52.2 all-gather.8
  156.5 51.7 all-gather.10
  475.6 53.2 reduce-scatter.15
  533.5 62.4 reduce-scatter.9
  600.6 89.0 reduce-scatter.7
  694.9 110.8 reduce-scatter.11
  810.5 111.1 reduce-scatter.13
where the time goes:
time: 939 us; the launch traced here: 928 us
  waiting for transfers between devices  584 us (62%)
  matrix products  100 us (11%)
  local copies, waits for them, and re-layouts  89.9 us (10%)
  other arithmetic  81.8 us (9%)
  blocking collectives  39.3 us (4%)
  between operations  14.3 us (2%)
  loops' own time  12.1 us (1%)
    reduce_scatter x1, waiting for transfers between devices, body(): lax.psum_scatter(summed[2][None], 'dp', scatter_dimension=1, tiled=True)  116 us
    reduce_scatter x1, waiting for transfers between devices, body(): lax.psum_scatter(summed[3][None], 'dp', scatter_dimension=1, tiled=True)  116 us
    reduce_scatter x1, waiting for transfers between devices, body(): lax.psum_scatter(summed[0][None], 'dp', scatter_dimension=2, tiled=True)  93.7 us
    all_gather x1, waiting for transfers between devices, body(): lax.all_gather(ff_up, 'dp', axis=1, tiled=True)  54.5 us
    all_gather x1, waiting for transfers between devices, body(): lax.all_gather(ff_down, 'dp', axis=1, tiled=True)  54 us
    all_gather x1, waiting for transfers between devices, body(): lax.all_gather(attn_in, 'dp', axis=2, tiled=True)  48.5 us
    psum x1, blocking collectives, body(): router_grad = lax.psum(router_total, ('section', 'dp'))  39.3 us
    all_gather x1, waiting for transfers between devices, body(): lax.all_gather(attn_out, 'dp', axis=1, tiled=True)  38 us
  transfers between devices with their start and end apart: 13, of which 10 were waited for; matrix products, arithmetic and copies ran while one was open for 18% of the time, Pallas kernels for 0%

commit v1 on v0

v1 whole, which is shorter than its diff:
```python
import jax
import jax.numpy as jnp
from jax import lax
from jax.sharding import PartitionSpec as P

HEAD_DIM = 64
EXACT = lax.Precision.HIGHEST
EPSILON = 1e-05
MASKED = -1e30
BF = jnp.bfloat16
F32 = jnp.float32


def move(value, pairs):
    return lax.ppermute(value, "dp", pairs)


def routes(n):
    depth = n // 4
    across = [(i, i ^ 2) for i in range(n)]
    beside = [(i, i ^ 1) for i in range(n)]
    shifts = [[(i, ((i // 4 + k) % depth) * 4 + i % 4) for i in range(n)] for k in range(depth)]
    return depth, across, beside, shifts


def after(value, token):
    return lax.optimization_barrier((value, token))[0]


def gather_parts(parts):
    n = lax.axis_size("dp")
    if n != 16:
        return [lax.all_gather(part, "dp", axis=0) for part in parts]
    depth, across, beside, shifts = routes(n)
    me = lax.axis_index("dp")
    own_across = [move(part, across) for part in parts]
    wholes, last = [], None
    for part, crossed in zip(parts, own_across):
        column = [part]
        for k in range(1, depth):
            source = part if last is None else after(part, last[k - 1][:1, :1])
            column.append(move(source, shifts[k]))
        last = column[1:]
        plane = [column, [crossed] + [move(held, across) for held in last]]
        whole = jnp.zeros((n,) + part.shape, part.dtype)
        for j in range(2):
            for k in range(depth):
                held = plane[j][k]
                for c, piece in ((0, held), (1, move(held, beside))):
                    origin = ((me // 4 - k) % depth) * 4 + ((me % 4) ^ (2 * j + c))
                    whole = lax.dynamic_update_index_in_dim(whole, piece, origin, 0)
        wholes.append(whole)
    return wholes


def scatter_sum(whole):
    n = lax.axis_size("dp")
    if n != 16:
        return lax.psum_scatter(whole.astype(F32), "dp", scatter_dimension=0, tiled=False)
    depth, across, beside, shifts = routes(n)
    me = lax.axis_index("dp")

    def piece(k, j, c):
        target = ((me // 4 + k) % depth) * 4 + ((me % 4) ^ (2 * j + c))
        return lax.dynamic_index_in_dim(whole, target, 0, keepdims=False)

    order = list(range(1, depth)) + [0]
    came = {}
    for j in (1, 0):
        got = move(jnp.stack([piece(k, j, 1) for k in order]), beside)
        for slot, k in enumerate(order):
            came[k, j] = got[slot].astype(F32) + piece(k, j, 0).astype(F32)
    crossed = {k: move(came[k, 1].astype(BF), across) for k in order}
    here = {k: came[k, 0] + crossed[k].astype(F32) for k in order}
    total = here[0]
    arrived = [move(here[k].astype(BF), shifts[k]) for k in range(1, depth)]
    for value in arrived:
        total = total + value.astype(F32)
    return total


def normalize(rows, gain):
    inverse = lax.rsqrt(jnp.mean(rows * rows, axis=-1, keepdims=True) + EPSILON)
    normed = rows * inverse
    return (normed, inverse, normed * gain)


def norm_back(upstream, normed, inverse, gain):
    scaled = upstream * gain
    d_gain = jnp.sum(upstream * normed, axis=(0, 1))
    d_rows = inverse * (scaled - normed * jnp.mean(scaled * normed, axis=-1, keepdims=True))
    return (d_rows, d_gain)


def gelu_exact(value):
    return jax.nn.gelu(value, approximate=False)


def segment_mask(segment):
    order = lax.iota(jnp.int32, segment.shape[1])
    return (order[None, :, None] >= order[None, None, :]) & (
        segment[:, :, None] == segment[:, None, :]
    )


def masked_scores(query, keyed, mask):
    scores = jnp.einsum(
        "sqhd,skhd->shqk", query, keyed, preferred_element_type=F32
    ) * HEAD_DIM ** (-0.5)
    return jnp.where(mask[:, None], scores, MASKED)


def block_forward(rows, mask, gains, w_in, w_out, w_up, w_down):
    batch, count, width = rows.shape
    normed_one, inverse_one, pre_one = normalize(rows, gains[0])
    act_one = pre_one.astype(BF)
    projected = jnp.einsum("srd,cde->csre", act_one, w_in, preferred_element_type=F32).astype(BF)
    heads = projected.reshape(3, batch, count, width // HEAD_DIM, HEAD_DIM)
    scores = masked_scores(heads[0], heads[1], mask)
    top = jnp.max(scores, axis=-1, keepdims=True)
    powers = jnp.exp(scores - top)
    total = jnp.sum(powers, axis=-1, keepdims=True)
    chances = (powers / total).astype(BF)
    mixed = jnp.einsum("shqk,skhd->sqhd", chances, heads[2], preferred_element_type=F32)
    mixed = mixed.reshape(batch, count, width).astype(BF)
    attended = jnp.einsum("srd,de->sre", mixed, w_out, preferred_element_type=F32)
    middle = rows + attended
    normed_two, inverse_two, pre_two = normalize(middle, gains[1])
    act_two = pre_two.astype(BF)
    upped = jnp.einsum("srd,df->srf", act_two, w_up, preferred_element_type=F32)
    hidden = gelu_exact(upped).astype(BF)
    branch = attended + jnp.einsum("srf,fd->srd", hidden, w_down, preferred_element_type=F32)
    log_total = top + jnp.log(total)
    first = (normed_one, inverse_one, act_one, heads, log_total, mixed)
    second = (normed_two, inverse_two, act_two, upped, hidden)
    return branch, first, second


def feed_back(grad_branch, second, gain, w_up, w_down):
    normed_two, inverse_two, act_two, upped, hidden = second
    d_out = grad_branch.astype(BF)
    d_hidden = jnp.einsum("srd,fd->srf", d_out, w_down, preferred_element_type=F32)
    d_upped = jax.vjp(gelu_exact, upped)[1](d_hidden)[0].astype(BF)
    d_act_two = jnp.einsum("srf,df->srd", d_upped, w_up, preferred_element_type=F32)
    d_middle, g_gain = norm_back(d_act_two, normed_two, inverse_two, gain)
    return d_middle, g_gain, (hidden, d_out, act_two, d_upped)


def attend_back(grad_branch, d_middle, mask, first, gain, w_in, w_out):
    normed_one, inverse_one, act_one, heads, log_total, mixed = first
    batch, count, width = grad_branch.shape
    d_attended = (grad_branch + d_middle).astype(BF)
    d_mixed = jnp.einsum("sre,de->srd", d_attended, w_out, preferred_element_type=F32).astype(BF)
    d_mixed = d_mixed.reshape(batch, count, width // HEAD_DIM, HEAD_DIM)
    chances = jnp.exp(masked_scores(heads[0], heads[1], mask) - log_total)
    d_chances = jnp.einsum("sqhd,skhd->shqk", d_mixed, heads[2], preferred_element_type=F32)
    d_value = jnp.einsum("shqk,sqhd->skhd", chances.astype(BF), d_mixed, preferred_element_type=F32)
    d_scores = chances * (d_chances - jnp.sum(chances * d_chances, axis=-1, keepdims=True))
    d_scores = d_scores.astype(BF)
    factor = HEAD_DIM ** (-0.5)
    d_query = jnp.einsum("shqk,skhd->sqhd", d_scores, heads[1], preferred_element_type=F32) * factor
    d_key = jnp.einsum("shqk,sqhd->skhd", d_scores, heads[0], preferred_element_type=F32) * factor
    d_projected = jnp.stack([d_query, d_key, d_value]).reshape(3, batch, count, width).astype(BF)
    d_act_one = jnp.einsum("csre,cde->srd", d_projected, w_in, preferred_element_type=F32)
    d_rows, g_gain = norm_back(d_act_one, normed_one, inverse_one, gain)
    return d_rows + d_middle, g_gain, (mixed, d_attended, act_one, d_projected)


def feed_grads(kept):
    hidden, d_out, act_two, d_upped = kept
    g_down = jnp.einsum("srf,srd->fd", hidden, d_out, preferred_element_type=F32)
    g_up = jnp.einsum("srd,srf->df", act_two, d_upped, preferred_element_type=F32)
    return g_up.astype(BF), g_down.astype(BF)


def attend_grads(kept):
    mixed, d_attended, act_one, d_projected = kept
    g_out = jnp.einsum("srd,sre->de", mixed, d_attended, preferred_element_type=F32)
    g_in = jnp.einsum("srd,csre->cde", act_one, d_projected, preferred_element_type=F32)
    return g_in.astype(BF), g_out.astype(BF)


def zeros_of(work, *operands):
    return jax.tree.map(lambda leaf: jnp.zeros(leaf.shape, leaf.dtype), jax.eval_shape(work, *operands))


def on_section(active, work, *operands):
    return lax.cond(active, work, lambda *inner: zeros_of(work, *inner), *operands)


def body(
    tokens, cotangent, segments, chosen, router, norm_gains, attn_in, attn_out, ff_up, ff_down
):
    n = lax.axis_size("dp")
    routed = lax.axis_index("section") == 0
    batch, length = segments.shape
    width = tokens.shape[1]
    kept = chosen.shape[1]
    rows_in, rows_down, ff = attn_in.shape[2], ff_down.shape[1], ff_up.shape[2]
    blocks = ff // width
    gains = norm_gains[0]

    first_part = jnp.concatenate([attn_in[0].reshape(-1, width), attn_out[0]])
    second_part = jnp.concatenate([ff_up[0][:, b * width:(b + 1) * width] for b in range(blocks)])
    whole_first, whole_second, whole_down = gather_parts([first_part, second_part, ff_down[0]])
    whole_first = whole_first.reshape(n, 4, rows_in, width).transpose(1, 0, 2, 3).reshape(4, -1, width)
    w_in, w_out = whole_first[:3], whole_first[3]
    w_up = whole_second.reshape(n, blocks, rows_in, width).transpose(0, 2, 1, 3).reshape(-1, ff)
    w_down = whole_down.reshape(-1, width)

    inputs = tokens.reshape(batch, length, width)
    upstream = cotangent.reshape(batch, length, width)
    picks = (chosen[:, :, None] == lax.iota(jnp.int32, length)[None, None, :]).astype(BF)

    def pick(rows):
        return jnp.einsum("wgo,woq->wgq", picks, rows, preferred_element_type=F32)

    def put(rows):
        return jnp.einsum("wgo,wgq->woq", picks, rows, preferred_element_type=F32)

    pick_mask = segment_mask(jnp.take_along_axis(segments, chosen, axis=1))

    def routed_forward():
        rows = pick(inputs)
        gate = jax.nn.sigmoid(jnp.einsum("skd,d->sk", rows, router, precision=EXACT))
        branch, first, second = block_forward(rows, pick_mask, gains, w_in, w_out, w_up, w_down)
        return (gate[..., None] * branch).astype(BF), (rows, gate, branch, first, second)

    delta, stash = on_section(routed, routed_forward)
    arrived = lax.ppermute(delta, "section", [(0, 1)])

    def dense_work():
        base = inputs.astype(F32) + put(arrived)
        mask = segment_mask(segments)
        branch, first, second = block_forward(base, mask, gains, w_in, w_out, w_up, w_down)
        grad = upstream.astype(F32)
        d_middle, g_two, kept_feed = feed_back(grad, second, gains[1], w_up, w_down)
        d_rows, g_one, kept_attend = attend_back(grad, d_middle, mask, first, gains[0], w_in, w_out)
        back = (grad + d_rows).astype(BF)
        result = (base + branch).astype(BF)
        return result, back, pick(back).astype(BF), jnp.stack([g_one, g_two]), kept_feed, kept_attend

    result, back, back_rows, g_gains, kept_feed, kept_attend = on_section(
        jnp.logical_not(routed), dense_work
    )
    d_delta = lax.ppermute(back_rows, "section", [(1, 0)])
    returned = lax.ppermute(back, "section", [(1, 0)])

    def routed_feed():
        rows, gate, branch, first, second = stash
        grad = gate[..., None] * d_delta.astype(F32)
        d_middle, g_two, kept_here = feed_back(grad, second, gains[1], w_up, w_down)
        return feed_grads(kept_here) + (d_middle, g_two)

    def dense_feed():
        return feed_grads(kept_feed) + (jnp.zeros((batch, kept, width), F32), g_gains[1])

    g_up, g_down, d_middle, g_two = lax.cond(routed, routed_feed, dense_feed)

    def routed_attend():
        rows, gate, branch, first, second = stash
        d_rows_out = d_delta.astype(F32)
        d_logit = jnp.sum(d_rows_out * branch, axis=-1) * gate * (1.0 - gate)
        d_picked, g_one, kept_here = attend_back(
            gate[..., None] * d_rows_out, d_middle, pick_mask, first, gains[0], w_in, w_out
        )
        d_picked = d_picked + d_logit[..., None] * router
        g_router = jnp.einsum("sk,skd->d", d_logit, rows, precision=EXACT)
        return attend_grads(kept_here) + (g_one, g_router, d_picked)

    def dense_attend():
        return attend_grads(kept_attend) + (
            g_gains[0], jnp.zeros_like(router), jnp.zeros((batch, kept, width), F32)
        )

    g_in, g_out, g_one, g_router, d_picked = lax.cond(routed, routed_attend, dense_attend)

    down_grad = scatter_sum(g_down.reshape(n, rows_down, width))
    up_grad = scatter_sum(
        g_up.reshape(n, rows_in, blocks, width).transpose(0, 2, 1, 3).reshape(n, -1, width)
    )
    attend_sum = scatter_sum(
        jnp.concatenate([g_in, g_out[None]])
        .reshape(4, n, rows_in, width).transpose(1, 0, 2, 3).reshape(n, -1, width)
    )
    gain_grad = lax.psum_scatter(jnp.stack([g_one, g_two]), "dp", scatter_dimension=1, tiled=True)
    router_grad = lax.psum(g_router, ("section", "dp"))

    spread = jnp.einsum("wgo,wgq->woq", picks.astype(F32), d_picked, precision=EXACT)
    first_rows = (returned.astype(F32) + spread).astype(BF)
    ends = jnp.where(routed, first_rows, result).reshape(1, -1, width)
    attend_sum = attend_sum.reshape(4, rows_in, width)
    up_grad = up_grad.reshape(blocks, rows_in, width).transpose(1, 0, 2).reshape(rows_in, ff)
    return (
        ends, router_grad, gain_grad[None], attend_sum[:3][None], attend_sum[3][None],
        up_grad[None], down_grad[None],
    )


def solution(mesh):
    return jax.shard_map(
        body,
        mesh=mesh,
        in_specs=(
            P("dp", None),
            P("dp", None),
            P("dp", None),
            P("dp", None),
            P(),
            P("section", None, None),
            P("section", None, "dp", None),
            P("section", "dp", None),
            P("section", "dp", None),
            P("section", "dp", None),
        ),
        out_specs=(
            P("section", "dp", None),
            P(),
            P("section", None, "dp"),
            P("section", None, "dp", None),
            P("section", "dp", None),
            P("section", "dp", None),
            P("section", "dp", None),
        ),
        check_vma=False,
    )
```

time: 939 us -> 614 us (0.65)
  waiting for transfers between devices: 584 us -> 223 us
  starting transfers between devices: 6.13 us -> 77.7 us
  matrix products: 100 us -> 53.8 us
  local copies, waits for them, and re-layouts: 89.9 us -> 131 us
  other arithmetic: 81.8 us -> 45 us
  blocking collectives: 39.3 us -> 52.1 us
    reduce_scatter x4 -> x0, waiting for transfers between devices: 349 us -> none  [the longest x1 116 us: body(): lax.psum_scatter(summed[2][None], 'dp', scatter_dimension=1, tiled=True)]
    all_gather x4 -> x0, waiting for transfers between devices: 195 us -> none  [the longest x1 54.5 us: body(): lax.all_gather(ff_up, 'dp', axis=1, tiled=True)]
    ppermute x4 -> x75, waiting for transfers between devices: 37.7 us -> 223 us  [the longest x72 129 us: move(): return lax.ppermute(value, 'dp', pairs)]
    ppermute x4 -> x75, starting transfers between devices: 5.77 us -> 77.7 us  [the longest x72 73.2 us: move(): return lax.ppermute(value, 'dp', pairs)]
    broadcast_in_dim x7 -> x1, other arithmetic: 55.5 us -> 2.08 us  [body(): down_grad[None]]
    dot_general x56 -> x23, matrix products: 100 us -> 53.8 us  [the longest x1 5.65 us: block_forward(): upped = jnp.einsum('srd,df->srf', act_two, w_up, preferred_element_type=F32)]
    dynamic_update_slice x0 -> x46, local copies, waits for them, and re-layouts: none -> 34.4 us  [gather_parts(): whole = lax.dynamic_update_index_in_dim(whole, piece, origin, 0)]
    cond x156 -> x25, local copies, waits for them, and re-layouts: 21.3 us -> 7.33 us  [the longest x1 6.65 us: body(): g_up, g_down, d_middle, g_two = lax.cond(routed, routed_feed, dense_feed)]
  transfers between devices with their start and end apart: 13 -> 76, of which waited for: 10 -> 22; matrix products, arithmetic and copies ran while one was open for 18% -> 28% of each run, Pallas kernels for 0% -> 0%
where the time goes in v1:
time: 614 us; the launch traced here: 604 us
  waiting for transfers between devices  223 us (36%)
  local copies, waits for them, and re-layouts  131 us (21%)
  starting transfers between devices  77.7 us (13%)
  matrix products  53.8 us (9%)
  blocking collectives  52.1 us (8%)
  other arithmetic  45 us (7%)
  between operations  15 us (2%)
    ppermute x72, waiting for transfers between devices, move(): return lax.ppermute(value, 'dp', pairs)  129 us
    ppermute x1, waiting for transfers between devices, body(): d_delta = lax.ppermute(back_rows, 'section', [(1, 0)])  91.4 us
    ppermute x72, starting transfers between devices, move(): return lax.ppermute(value, 'dp', pairs)  73.2 us
    psum x1, blocking collectives, body(): router_grad = lax.psum(g_router, ('section', 'dp'))  52.1 us
    dynamic_update_slice x46, local copies, waits for them, and re-layouts, gather_parts(): whole = lax.dynamic_update_index_in_dim(whole, piece, origin, 0)  34.4 us
    another operation x17, local copies, waits for them, and re-layouts  21.1 us
    unnamed x58, local copies, waits for them, and re-layouts  13.8 us
  transfers between devices with their start and end apart: 76, of which 22 were waited for; matrix products, arithmetic and copies ran while one was open for 28% of the time, Pallas kernels for 0%

profile of v1, /device:TPU:0, one launch (start us, length us, event | category | flops | bytes accessed | tf_op | source)
XLA Modules:
  0.0 603.9 jit_solution(6359061449312085723)
XLA Ops:
  10.3 5.1 collective-permute-start.20
  37.2 6.5 %collective-permute-done.1 = bf16[192,768]{1,0:T(8,128)(2,1)S(1)} collective-permute-done((bf16[192,768]{1,0:T(8,128)(2,1)S(1)}, bf16[192,768]{1,0:T(8,128)(2,1)S(1)}, u32[]{:S(2)}, u32[]{:S(2)}) %collective-permute-start.1) | collective-permute-done | bytes 294944 | tf_op jit(solution)/shard_map/ppermute | solution.py:15
  49.2 4.2 collective-permute-done.31
  53.4 4.1 collective-permute-start.5
  61.1 14.9 %collective-permute-done.3 = bf16[192,768]{1,0:T(8,128)(2,1)S(1)} collective-permute-done((bf16[192,768]{1,0:T(8,128)(2,1)S(1)}, bf16[192,768]{1,0:T(8,128)(2,1)S(1)}, u32[]{:S(2)}, u32[]{:S(2)}) %collective-permute-start.3) | collective-permute-done | bytes 294944 | tf_op jit(solution)/shard_map/ppermute | solution.py:15
  88.2 14.5 %collective-permute-done.33 = bf16[192,768]{1,0:T(8,128)(2,1)S(1)} collective-permute-done((bf16[192,768]{1,0:T(8,128)(2,1)S(1)}, bf16[192,768]{1,0:T(8,128)(2,1)S(1)}, u32[]{:S(2)}, u32[]{:S(2)}) %collective-permute-start.33) | collective-permute-done | bytes 294944 | tf_op jit(solution)/shard_map/ppermute | solution.py:15
  114.6 10.6 %collective-permute-done.24 = bf16[192,768]{1,0:T(8,128)(2,1)S(1)} collective-permute-done((bf16[192,768]{1,0:T(8,128)(2,1)S(1)}, bf16[192,768]{1,0:T(8,128)(2,1)S(1)}, u32[]{:S(2)}, u32[]{:S(2)}) %collective-permute-start.24) | collective-permute-done | bytes 294944 | tf_op jit(solution)/shard_map/ppermute | solution.py:15
  125.9 10.8 %collective-permute-done.9 = bf16[192,768]{1,0:T(8,128)(2,1)S(1)} collective-permute-done((bf16[192,768]{1,0:T(8,128)(2,1)S(1)}, bf16[192,768]{1,0:T(8,128)(2,1)S(1)}, u32[]{:S(2)}, u32[]{:S(2)}) %collective-permute-start.9) | collective-permute-done | bytes 294944 | tf_op jit(solution)/shard_map/ppermute | solution.py:15
  138.6 5.9 collective-permute-done.39
  159.8 4.4 collective-permute-done.41
  182.5 34.3 %conditional.4 = (bf16[2,32,768]{2,1,0:T(8,128)(2,1)}, f32[2,32,768]{2,1,0:T(8,128)}, f32[2,32]{1,0:T(2,128)}, f32[2,32,768]{2,1,0:T(8,128)}, f32[2,32,768]{2,1,...) conditional(s32[]{:T(128)} %convert_element_type.530, () %tuple.57, ...), branch_computations={%region_0.1_spmd, %region_1.6_spmd} | conditional | flops 951877184 | bytes 23093880 | solution.py:188
  204.8 5.7 fusion.22
  220.9 19.0 %conditional.5 = (bf16[2,256,768]{2,1,0:T(8,128)(2,1)}, bf16[2,256,768]{2,1,0:T(8,128)(2,1)}, bf16[2,32,768]{2,1,0:T(8,128)(2,1)}, f32[2,768]{1,0:T(2,128)}, bf1...) conditional(s32[]{:T(128)} %convert_element_type.528, () %tuple.56, ...), branch_computations={%region_6.7_spmd, %region_7.17_spmd} | conditional | flops 15931119616 | bytes 350218240 | solution.py:188
  242.6 91.4 %collective-permute-done.47 = bf16[2,32,768]{2,1,0:T(8,128)(2,1)S(1)} collective-permute-done((bf16[2,32,768]{2,1,0:T(8,128)(2,1)}, bf16[2,32,768]{2,1,0:T(8,128)(2,1)S(1)}, u32[]{:S(2)}, u32[]{:S(2)}) %collective-permute-start.47) | collective-permute-done | bytes 98336 | tf_op jit(solution)/shard_map/ppermute | solution.py:246
  334.6 43.0 %conditional.6 = (f32[2,32,768]{2,1,0:T(8,128)}, bf16[16,192,768]{2,1,0:T(8,128)(2,1)}, f32[1,768]{1,0:T(1,128)S(1)}, bf16[16,48,4,768]{3,2,1,0:T(4,128)(2,1)}) conditional(s32[]{:T(128)} %convert_element_type.530, (bf16[2,256,768]{2,1,0:T(8,128)(2,1)}, bf16[2,256,3072]{2,1,0:T(8,128)(2,1)}, bf16[2,256,3072]{2,1,0:T(8,128)(2,1)}, ...), branch_computations={%region_17.18_spmd, %region_18.21_spmd} | conditional | flops 4836556800 | bytes 71700400 | solution.py:258
  334.8 5.4 fusion.91
  345.2 4.7 fusion.86
  349.9 6.6 %copy.167 = bf16[3072,768]{1,0:T(8,128)(2,1)} copy(bf16[3072,768]{0,1:T(8,128)(2,1)} %fusion.86) | data formatting | bytes 9437184 | tf_op jit(solution)/shard_map/cond/branch_1_fun/convert_element_type | solution.py:173
  356.5 4.7 fusion.85
  361.2 6.7 %copy.211 = bf16[768,3072]{1,0:T(8,128)(2,1)} copy(bf16[768,3072]{0,1:T(8,128)(2,1)} %fusion.85) | data formatting | bytes 9437184 | tf_op jit(solution)/shard_map/cond | solution.py:258
  367.9 9.8 %reshape.428 = bf16[16,48,4,768]{3,2,1,0:T(4,128)(2,1)} reshape(bf16[768,3072]{1,0:T(8,128)(2,1)} %copy.211) | data formatting | bytes 9437184 | tf_op jit(solution)/shard_map/reshape | solution.py:280
  378.2 33.8 %conditional.7 = (f32[768]{0:T(1024)}, f32[2,32,768]{2,1,0:T(8,128)}, bf16[3,16,48,768]{3,2,1,0:T(8,128)(2,1)S(1)}, bf16[1,16,48,768]{3,2,1,0:T(8,128)(2,1)S(1)}, f32[1,768]{1,0:T(1,128)S(1)}) conditional(s32[]{:T(128)} %convert_element_type.530, (bf16[3,2,256,768]{3,2,0,1:T(8,128)(2,1)}, bf16[2,256,768]{2,1,0:T(8,128)(2,1)}, ...), branch_computations={%region_21.22_spmd, %region_22.27_spmd} | conditional | flops 2418278400 | bytes 20441324 | solution.py:276
  438.2 52.1 %psum.7 = f32[768]{0:T(1024)} all-reduce(f32[768]{0:T(1024)} %get-tuple-element.243), channel_id=1, replica_groups=mesh['section'=2,'dp'=16] {'section','dp'}, use_global_device_ids=true, to_apply=%region_27.28 | all-reduce | flops 768 | bytes 6144 | tf_op jit(solution)/shard_map/psum | solution.py:287
  505.8 4.3 collective-permute-done.64
  512.2 4.3 collective-permute-done.62
  516.5 6.3 %collective-permute-done.60 = bf16[192,768]{1,0:T(8,128)(2,1)S(1)} collective-permute-done((bf16[192,768]{1,0:T(8,128)(2,1)S(1)}, bf16[192,768]{1,0:T(8,128)(2,1)S(1)}, u32[]{:S(2)}, u32[]{:S(2)}) %collective-permute-start.60) | collective-permute-done | bytes 294944 | tf_op jit(solution)/shard_map/ppermute | solution.py:15
  530.9 4.6 collective-permute-done.71
  537.4 4.3 collective-permute-done.69
  553.8 5.3 collective-permute-start.74
  559.0 9.5 %collective-permute-start.72 = (bf16[192,768]{1,0:T(8,128)(2,1)S(1)}, bf16[192,768]{1,0:T(8,128)(2,1)S(1)}, u32[]{:S(2)}, u32[]{:S(2)}) collective-permute-start(bf16[192,768]{1,0:T(8,128)(2,1)S(1)} %get-tuple-element.487), channel_id=1, source_target_pairs={{0,8},{1,9},{2,10},{3,11},{4,12},{5,13},{6,14},{7,15},{8,0},{9,1},... | collective-permute-start | bytes 884744 | tf_op jit(solution)/shard_map/ppermute | solution.py:15
  568.6 15.1 %collective-permute-done.63 = bf16[192,768]{1,0:T(8,128)(2,1)S(1)} collective-permute-done((bf16[192,768]{1,0:T(8,128)(2,1)S(1)}, bf16[192,768]{1,0:T(8,128)(2,1)S(1)}, u32[]{:S(2)}, u32[]{:S(2)}) %collective-permute-start.63) | collective-permute-done | bytes 294944 | tf_op jit(solution)/shard_map/ppermute | solution.py:15
  587.9 6.6 %collective-permute-done.72 = bf16[192,768]{1,0:T(8,128)(2,1)S(1)} collective-permute-done((bf16[192,768]{1,0:T(8,128)(2,1)S(1)}, bf16[192,768]{1,0:T(8,128)(2,1)S(1)}, u32[]{:S(2)}, u32[]{:S(2)}) %collective-permute-start.72) | collective-permute-done | bytes 294944 | tf_op jit(solution)/shard_map/ppermute | solution.py:15
  (374 shorter events, 254.6 us)
Async XLA Ops:
  7.2 483.1 %reduce-scatter.4.cloned.1.call-start = ((), (), s32[]{:S(2)}) async-start(), calls=%async_computation.1 | async-start | bytes 417792
  10.3 68.6 %collective-permute-start.20 = (bf16[192,768]{1,0:T(8,128)(2,1)S(1)}, bf16[192,768]{1,0:T(8,128)(2,1)S(1)}, u32[]{:S(2)}, u32[]{:S(2)}) collective-permute-start(bf16[192,768]{1,0:T(8,128)(2,1)S(1)} %pad_maximum_fusion.12), channel_id=1, source_target_pairs={{0,12},{1,13},{2,14},{3,15},{4,0},{5,1},{6,2},{7,3},{8,4},{9,5},{1... | collective-permute-start | bytes 884744 | tf_op jit(solution)/shard_map/ppermute | solution.py:15
  15.4 43.6 %collective-permute-start.18 = (bf16[192,768]{1,0:T(8,128)(2,1)S(1)}, bf16[192,768]{1,0:T(8,128)(2,1)S(1)}, u32[]{:S(2)}, u32[]{:S(2)}) collective-permute-start(bf16[192,768]{1,0:T(8,128)(2,1)S(1)} %pad_maximum_fusion.12), channel_id=1, source_target_pairs={{0,8},{1,9},{2,10},{3,11},{4,12},{5,13},{6,14},{7,15},{8,0},{9,1},... | collective-permute-start | bytes 884744 | tf_op jit(solution)/shard_map/ppermute | solution.py:15
  15.4 21.0 %collective-permute-start.16 = (bf16[192,768]{1,0:T(8,128)(2,1)S(1)}, bf16[192,768]{1,0:T(8,128)(2,1)S(1)}, u32[]{:S(2)}, u32[]{:S(2)}) collective-permute-start(bf16[192,768]{1,0:T(8,128)(2,1)S(1)} %pad_maximum_fusion.12), channel_id=1, source_target_pairs={{0,4},{1,5},{2,6},{3,7},{4,8},{5,9},{6,10},{7,11},{8,12},{9,13},{1... | collective-permute-start | bytes 884744 | tf_op jit(solution)/shard_map/ppermute | solution.py:15
  30.9 73.0 %collective-permute-start.22 = (bf16[192,768]{1,0:T(8,128)(2,1)S(1)}, bf16[192,768]{1,0:T(8,128)(2,1)S(1)}, u32[]{:S(2)}, u32[]{:S(2)}) collective-permute-start(bf16[192,768]{1,0:T(8,128)(2,1)S(1)} %pad_maximum_fusion.12), channel_id=1, source_target_pairs={{0,2},{1,3},{2,0},{3,1},{4,6},{5,7},{6,4},{7,5},{8,10},{9,11},{10,... | collective-permute-start | bytes 884744 | tf_op jit(solution)/shard_map/ppermute | solution.py:15
  53.4 29.8 %collective-permute-start.5 = (bf16[192,768]{1,0:T(8,128)(2,1)S(1)}, bf16[192,768]{1,0:T(8,128)(2,1)S(1)}, u32[]{:S(2)}, u32[]{:S(2)}) collective-permute-start(bf16[192,768]{1,0:T(8,128)(2,1)S(1)} %pad_maximum_fusion.11), channel_id=1, source_target_pairs={{0,12},{1,13},{2,14},{3,15},{4,0},{5,1},{6,2},{7,3},{8,4},{9,5},{1... | collective-permute-start | bytes 884744 | tf_op jit(solution)/shard_map/ppermute | solution.py:15
  75.9 28.6 %collective-permute-start.7 = (bf16[192,768]{1,0:T(8,128)(2,1)S(1)}, bf16[192,768]{1,0:T(8,128)(2,1)S(1)}, u32[]{:S(2)}, u32[]{:S(2)}) collective-permute-start(bf16[192,768]{1,0:T(8,128)(2,1)S(1)} %pad_maximum_fusion.11), channel_id=1, source_target_pairs={{0,2},{1,3},{2,0},{3,1},{4,6},{5,7},{6,4},{7,5},{8,10},{9,11},{10,... | collective-permute-start | bytes 884744 | tf_op jit(solution)/shard_map/ppermute | solution.py:15
  78.9 28.8 %collective-permute-start.35 = (bf16[192,768]{1,0:T(8,128)(2,1)S(1)}, bf16[192,768]{1,0:T(8,128)(2,1)S(1)}, u32[]{:S(2)}, u32[]{:S(2)}) collective-permute-start(bf16[192,768]{1,0:T(8,128)(2,1)S(1)} %bitcast.560), channel_id=1, source_target_pairs={{0,12},{1,13},{2,14},{3,15},{4,0},{5,1},{6,2},{7,3},{8,4},{9,5},{1... | collective-permute-start | bytes 884744 | tf_op jit(solution)/shard_map/ppermute | solution.py:15
  86.9 26.3 %collective-permute-start.37 = (bf16[192,768]{1,0:T(8,128)(2,1)S(1)}, bf16[192,768]{1,0:T(8,128)(2,1)S(1)}, u32[]{:S(2)}, u32[]{:S(2)}) collective-permute-start(bf16[192,768]{1,0:T(8,128)(2,1)S(1)} %bitcast.562), channel_id=1, source_target_pairs={{0,2},{1,3},{2,0},{3,1},{4,6},{5,7},{6,4},{7,5},{8,10},{9,11},{10,... | collective-permute-start | bytes 884744 | tf_op jit(solution)/shard_map/ppermute | solution.py:15
  102.6 51.6 %collective-permute-start.28 = (bf16[192,768]{1,0:T(8,128)(2,1)S(1)}, bf16[192,768]{1,0:T(8,128)(2,1)S(1)}, u32[]{:S(2)}, u32[]{:S(2)}) collective-permute-start(bf16[192,768]{1,0:T(8,128)(2,1)S(1)} %collective-permute-done.20), channel_id=1, source_target_pairs={{0,2},{1,3},{2,0},{3,1},{4,6},{5,7},{6,4},{7,5},{8,10},{9,11},{10,... | collective-permute-start | bytes 884744 | tf_op jit(solution)/shard_map/ppermute | solution.py:15
  104.6 41.9 %collective-permute-start.26 = (bf16[192,768]{1,0:T(8,128)(2,1)S(1)}, bf16[192,768]{1,0:T(8,128)(2,1)S(1)}, u32[]{:S(2)}, u32[]{:S(2)}) collective-permute-start(bf16[192,768]{1,0:T(8,128)(2,1)S(1)} %collective-permute-done.18), channel_id=1, source_target_pairs={{0,2},{1,3},{2,0},{3,1},{4,6},{5,7},{6,4},{7,5},{8,10},{9,11},{10,... | collective-permute-start | bytes 884744 | tf_op jit(solution)/shard_map/ppermute | solution.py:15
  111.0 45.1 %collective-permute-start.13 = (bf16[192,768]{1,0:T(8,128)(2,1)S(1)}, bf16[192,768]{1,0:T(8,128)(2,1)S(1)}, u32[]{:S(2)}, u32[]{:S(2)}) collective-permute-start(bf16[192,768]{1,0:T(8,128)(2,1)S(1)} %collective-permute-done.5), channel_id=1, source_target_pairs={{0,2},{1,3},{2,0},{3,1},{4,6},{5,7},{6,4},{7,5},{8,10},{9,11},{10,... | collective-permute-start | bytes 884744 | tf_op jit(solution)/shard_map/ppermute | solution.py:15
  113.3 23.4 %collective-permute-start.9 = (bf16[192,768]{1,0:T(8,128)(2,1)S(1)}, bf16[192,768]{1,0:T(8,128)(2,1)S(1)}, u32[]{:S(2)}, u32[]{:S(2)}) collective-permute-start(bf16[192,768]{1,0:T(8,128)(2,1)S(1)} %collective-permute-done.1), channel_id=1, source_target_pairs={{0,2},{1,3},{2,0},{3,1},{4,6},{5,7},{6,4},{7,5},{8,10},{9,11},{10,... | collective-permute-start | bytes 884744 | tf_op jit(solution)/shard_map/ppermute | solution.py:15
  239.9 94.1 %collective-permute-start.47 = (bf16[2,32,768]{2,1,0:T(8,128)(2,1)}, bf16[2,32,768]{2,1,0:T(8,128)(2,1)S(1)}, u32[]{:S(2)}, u32[]{:S(2)}) collective-permute-start(bf16[2,32,768]{2,1,0:T(8,128)(2,1)} %get-tuple-element.221), channel_id=1, source_target_pairs={{16,0},{17,1},{18,2},{19,3},{20,4},{21,5},{22,6},{23,7},{24,8},{25... | collective-permute-start | bytes 294920 | tf_op jit(solution)/shard_map/ppermute | solution.py:246
  241.3 187.3 %collective-permute-start.46 = (bf16[2,256,768]{2,1,0:T(8,128)(2,1)}, bf16[2,256,768]{2,1,0:T(8,128)(2,1)}, u32[]{:S(2)}, u32[]{:S(2)}) collective-permute-start(bf16[2,256,768]{2,1,0:T(8,128)(2,1)} %get-tuple-element.215), channel_id=1, source_target_pairs={{16,0},{17,1},{18,2},{19,3},{20,4},{21,5},{22,6},{23,7},{24,8},{25... | collective-permute-start | bytes 2359304 | tf_op jit(solution)/shard_map/ppermute | solution.py:247
  428.5 65.0 %collective-permute-start.67 = (bf16[4,192,768]{2,1,0:T(8,128)(2,1)}, bf16[4,192,768]{2,1,0:T(8,128)(2,1)}, u32[]{:S(2)}, u32[]{:S(2)}) collective-permute-start(bf16[4,192,768]{2,1,0:T(8,128)(2,1)} %pad_maximum_fusion.10), channel_id=1, source_target_pairs={{0,1},{1,0},{2,3},{3,2},{4,5},{5,4},{6,7},{7,6},{8,9},{9,8},{10,11... | collective-permute-start | bytes 3538952 | tf_op jit(solution)/shard_map/ppermute | solution.py:15
  430.9 70.8 %collective-permute-start.66 = (bf16[4,192,768]{2,1,0:T(8,128)(2,1)}, bf16[4,192,768]{2,1,0:T(8,128)(2,1)}, u32[]{:S(2)}, u32[]{:S(2)}) collective-permute-start(bf16[4,192,768]{2,1,0:T(8,128)(2,1)} %pad_maximum_fusion.9), channel_id=1, source_target_pairs={{0,1},{1,0},{2,3},{3,2},{4,5},{5,4},{6,7},{7,6},{8,9},{9,8},{10,11... | collective-permute-start | bytes 3538952 | tf_op jit(solution)/shard_map/ppermute | solution.py:15
  433.9 62.0 %collective-permute-start.55 = (bf16[192,768]{1,0:T(8,128)(2,1)}, bf16[192,768]{1,0:T(8,128)(2,1)}, u32[]{:S(2)}, u32[]{:S(2)}) collective-permute-start(bf16[192,768]{1,0:T(8,128)(2,1)} %get-tuple-element.496), channel_id=1, source_target_pairs={{0,2},{1,3},{2,0},{3,1},{4,6},{5,7},{6,4},{7,5},{8,10},{9,11},{10,... | collective-permute-start | bytes 884744 | tf_op jit(solution)/shard_map/ppermute | solution.py:15
  434.3 61.7 %collective-permute-start.53 = (bf16[192,768]{1,0:T(8,128)(2,1)}, bf16[192,768]{1,0:T(8,128)(2,1)}, u32[]{:S(2)}, u32[]{:S(2)}) collective-permute-start(bf16[192,768]{1,0:T(8,128)(2,1)} %get-tuple-element.497), channel_id=1, source_target_pairs={{0,2},{1,3},{2,0},{3,1},{4,6},{5,7},{6,4},{7,5},{8,10},{9,11},{10,... | collective-permute-start | bytes 884744 | tf_op jit(solution)/shard_map/ppermute | solution.py:15
  435.9 62.0 %collective-permute-start.51 = (bf16[192,768]{1,0:T(8,128)(2,1)S(1)}, bf16[192,768]{1,0:T(8,128)(2,1)}, u32[]{:S(2)}, u32[]{:S(2)}) collective-permute-start(bf16[192,768]{1,0:T(8,128)(2,1)S(1)} %get-tuple-element.498), channel_id=1, source_target_pairs={{0,2},{1,3},{2,0},{3,1},{4,6},{5,7},{6,4},{7,5},{8,10},{9,11},{10,... | collective-permute-start | bytes 884744 | tf_op jit(solution)/shard_map/ppermute | solution.py:15
  497.9 24.9 %collective-permute-start.60 = (bf16[192,768]{1,0:T(8,128)(2,1)S(1)}, bf16[192,768]{1,0:T(8,128)(2,1)S(1)}, u32[]{:S(2)}, u32[]{:S(2)}) collective-permute-start(bf16[192,768]{1,0:T(8,128)(2,1)S(1)} %get-tuple-element.491), channel_id=1, source_target_pairs={{0,2},{1,3},{2,0},{3,1},{4,6},{5,7},{6,4},{7,5},{8,10},{9,11},{10,... | collective-permute-start | bytes 884744 | tf_op jit(solution)/shard_map/ppermute | solution.py:15
  501.6 27.5 %collective-permute-start.73 = (bf16[192,768]{1,0:T(8,128)(2,1)S(1)}, bf16[192,768]{1,0:T(8,128)(2,1)S(1)}, u32[]{:S(2)}, u32[]{:S(2)}) collective-permute-start(bf16[192,768]{1,0:T(8,128)(2,1)S(1)} %get-tuple-element.482), channel_id=1, source_target_pairs={{0,2},{1,3},{2,0},{3,1},{4,6},{5,7},{6,4},{7,5},{8,10},{9,11},{10,... | collective-permute-start | bytes 884744 | tf_op jit(solution)/shard_map/ppermute | solution.py:15
  503.8 31.6 %collective-permute-start.71 = (bf16[192,768]{1,0:T(8,128)(2,1)S(1)}, bf16[192,768]{1,0:T(8,128)(2,1)S(1)}, u32[]{:S(2)}, u32[]{:S(2)}) collective-permute-start(bf16[192,768]{1,0:T(8,128)(2,1)S(1)} %get-tuple-element.483), channel_id=1, source_target_pairs={{0,2},{1,3},{2,0},{3,1},{4,6},{5,7},{6,4},{7,5},{8,10},{9,11},{10,... | collective-permute-start | bytes 884744 | tf_op jit(solution)/shard_map/ppermute | solution.py:15
  510.1 31.6 %collective-permute-start.69 = (bf16[192,768]{1,0:T(8,128)(2,1)S(1)}, bf16[192,768]{1,0:T(8,128)(2,1)S(1)}, u32[]{:S(2)}, u32[]{:S(2)}) collective-permute-start(bf16[192,768]{1,0:T(8,128)(2,1)S(1)} %get-tuple-element.484), channel_id=1, source_target_pairs={{0,2},{1,3},{2,0},{3,1},{4,6},{5,7},{6,4},{7,5},{8,10},{9,11},{10,... | collective-permute-start | bytes 884744 | tf_op jit(solution)/shard_map/ppermute | solution.py:15
  516.5 25.3 %collective-permute-start.52 = (bf16[192,768]{1,0:T(8,128)(2,1)S(1)}, bf16[192,768]{1,0:T(8,128)(2,1)S(1)}, u32[]{:S(2)}, u32[]{:S(2)}) collective-permute-start(bf16[192,768]{1,0:T(8,128)(2,1)S(1)} %get-tuple-element.499), channel_id=1, source_target_pairs={{0,4},{1,5},{2,6},{3,7},{4,8},{5,9},{6,10},{7,11},{8,12},{9,13},{1... | collective-permute-start | bytes 884744 | tf_op jit(solution)/shard_map/ppermute | solution.py:15
  522.8 22.8 %collective-permute-start.56 = (bf16[192,768]{1,0:T(8,128)(2,1)S(1)}, bf16[192,768]{1,0:T(8,128)(2,1)S(1)}, u32[]{:S(2)}, u32[]{:S(2)}) collective-permute-start(bf16[192,768]{1,0:T(8,128)(2,1)S(1)} %get-tuple-element.500), channel_id=1, source_target_pairs={{0,12},{1,13},{2,14},{3,15},{4,0},{5,1},{6,2},{7,3},{8,4},{9,5},{1... | collective-permute-start | bytes 884744 | tf_op jit(solution)/shard_map/ppermute | solution.py:15
  529.1 21.5 %collective-permute-start.54 = (bf16[192,768]{1,0:T(8,128)(2,1)S(1)}, bf16[192,768]{1,0:T(8,128)(2,1)S(1)}, u32[]{:S(2)}, u32[]{:S(2)}) collective-permute-start(bf16[192,768]{1,0:T(8,128)(2,1)S(1)} %get-tuple-element.501), channel_id=1, source_target_pairs={{0,8},{1,9},{2,10},{3,11},{4,12},{5,13},{6,14},{7,15},{8,0},{9,1},... | collective-permute-start | bytes 884744 | tf_op jit(solution)/shard_map/ppermute | solution.py:15
  545.6 38.1 %collective-permute-start.63 = (bf16[192,768]{1,0:T(8,128)(2,1)S(1)}, bf16[192,768]{1,0:T(8,128)(2,1)S(1)}, u32[]{:S(2)}, u32[]{:S(2)}) collective-permute-start(bf16[192,768]{1,0:T(8,128)(2,1)S(1)} %get-tuple-element.494), channel_id=1, source_target_pairs={{0,8},{1,9},{2,10},{3,11},{4,12},{5,13},{6,14},{7,15},{8,0},{9,1},... | collective-permute-start | bytes 884744 | tf_op jit(solution)/shard_map/ppermute | solution.py:15
  550.6 37.3 %collective-permute-start.68 = (bf16[192,768]{1,0:T(8,128)(2,1)S(1)}, bf16[192,768]{1,0:T(8,128)(2,1)S(1)}, u32[]{:S(2)}, u32[]{:S(2)}) collective-permute-start(bf16[192,768]{1,0:T(8,128)(2,1)S(1)} %get-tuple-element.481), channel_id=1, source_target_pairs={{0,2},{1,3},{2,0},{3,1},{4,6},{5,7},{6,4},{7,5},{8,10},{9,11},{10,... | collective-permute-start | bytes 884744 | tf_op jit(solution)/shard_map/ppermute | solution.py:15
  553.7 34.2 %collective-permute-start.70 = (bf16[192,768]{1,0:T(8,128)(2,1)}, bf16[192,768]{1,0:T(8,128)(2,1)S(1)}, u32[]{:S(2)}, u32[]{:S(2)}) collective-permute-start(bf16[192,768]{1,0:T(8,128)(2,1)} %get-tuple-element.485), channel_id=1, source_target_pairs={{0,4},{1,5},{2,6},{3,7},{4,8},{5,9},{6,10},{7,11},{8,12},{9,13},{1... | collective-permute-start | bytes 884744 | tf_op jit(solution)/shard_map/ppermute | solution.py:15
  553.8 34.1 %collective-permute-start.74 = (bf16[192,768]{1,0:T(8,128)(2,1)}, bf16[192,768]{1,0:T(8,128)(2,1)S(1)}, u32[]{:S(2)}, u32[]{:S(2)}) collective-permute-start(bf16[192,768]{1,0:T(8,128)(2,1)} %get-tuple-element.486), channel_id=1, source_target_pairs={{0,12},{1,13},{2,14},{3,15},{4,0},{5,1},{6,2},{7,3},{8,4},{9,5},{1... | collective-permute-start | bytes 884744 | tf_op jit(solution)/shard_map/ppermute | solution.py:15
  559.0 35.5 %collective-permute-start.72 = (bf16[192,768]{1,0:T(8,128)(2,1)S(1)}, bf16[192,768]{1,0:T(8,128)(2,1)S(1)}, u32[]{:S(2)}, u32[]{:S(2)}) collective-permute-start(bf16[192,768]{1,0:T(8,128)(2,1)S(1)} %get-tuple-element.487), channel_id=1, source_target_pairs={{0,8},{1,9},{2,10},{3,11},{4,12},{5,13},{6,14},{7,15},{8,0},{9,1},... | collective-permute-start | bytes 884744 | tf_op jit(solution)/shard_map/ppermute | solution.py:15
  (83 other events, 756.5 us)
Sparse Core Ops, SparseCore 0:
  429.8 55.8 reduce-scatter.3
